TPU v7x, 32 devices: a whole 2x2x4 slice. The times are simulated.
32 devices in a mesh: dp: 8 (over z, x), mp: 4 (over y, core).
Axes of the slice: x: 2, y: 2, z: 4, core: 2. Of those that a mesh axis runs over, the one named last changes fastest.
Arguments:
- layer_in: float32 [4096, 768], P(('dp', 'mp')), may hold values from -6 to 6
- node_counts: int32 [32], P('dp'), may hold values from 32 to 127, as said below
- spatial_ids: int32 [32, 128, 128], P('dp'), may hold values from 0 to 20
- path_ids: int32 [32, 5, 128, 128], P('dp'), may hold values from 0 to 1535
- ln1_gain: float32 [768], replicated, may hold values from 0.25 to 1.75
- ln1_bias: float32 [768], replicated, may hold values from -3 to 3
- w_q: bfloat16 [768, 768], P('dp', 'mp'), may hold values from -0.21875 to 0.21875
- w_k: bfloat16 [768, 768], P('dp', 'mp'), may hold values from -0.21875 to 0.21875
- w_v: bfloat16 [768, 768], P('dp', 'mp'), may hold values from -0.21875 to 0.21875
- q_bias: float32 [768], P('mp'), may hold values from -3 to 3
- v_bias: float32 [768], P('mp'), may hold values from -3 to 3
- spatial_table: bfloat16 [22, 32], replicated, may hold values from -4 to 4
- edge_table: bfloat16 [1536, 32], P('dp'), may hold values from -4 to 4
- w_o: bfloat16 [768, 768], P('dp', 'mp'), may hold values from -0.875 to 0.875
- o_bias: float32 [768], replicated, may hold values from -3 to 3
- ln2_gain: float32 [768], replicated, may hold values from 0.25 to 1.75
- ln2_bias: float32 [768], replicated, may hold values from -3 to 3
- w_in: bfloat16 [768, 768], P('dp', 'mp'), may hold values from -0.21875 to 0.21875
- in_bias: float32 [768], P('mp'), may hold values from -3 to 3
- w_out: bfloat16 [768, 768], P('dp', 'mp'), may hold values from -0.3125 to 0.3125
- out_bias: float32 [768], replicated, may hold values from -3 to 3
- cotangent: float32 [4096, 768], P(('dp', 'mp')), may hold values from -6 to 6
Outputs:
- layer_out: float32 [4096, 768], P(('dp', 'mp'))
- grad_layer_in: float32 [4096, 768], P(('dp', 'mp'))
- grad_ln1_gain: float32 [768], replicated
- grad_ln1_bias: float32 [768], replicated
- grad_w_q: float32 [768, 768], P('dp', 'mp')
- grad_w_k: float32 [768, 768], P('dp', 'mp')
- grad_w_v: float32 [768, 768], P('dp', 'mp')
- grad_q_bias: float32 [768], P('mp')
- grad_v_bias: float32 [768], P('mp')
- grad_spatial_table: float32 [22, 32], P(None, 'mp')
- grad_edge_table: float32 [1536, 32], P('dp', 'mp')
- grad_w_o: float32 [768, 768], P('dp', 'mp')
- grad_o_bias: float32 [768], replicated
- grad_ln2_gain: float32 [768], replicated
- grad_ln2_bias: float32 [768], replicated
- grad_w_in: float32 [768, 768], P('dp', 'mp')
- grad_in_bias: float32 [768], P('mp')
- grad_w_out: float32 [768, 768], P('dp', 'mp')
- grad_out_bias: float32 [768], replicated
Inputs may be any that keep to these rules, and one draw needn't show every extreme that they name: Graph g holds its virtual node in slot 0 and its nodes in slots 1 to node_counts[g]; later slots are padding. `spatial_ids`: bucket 22 - 2 stands for unreachable pairs; bucket 22 - 1 is never given.
All inputs are finite; a program needn't handle non-finite values.
Results may differ from a plain program's by a relative error of at most 0.012.
Values may be sent and summed in bfloat16 or wider, within the bound.
No kernel may reach another device: no remote copies, remote signals or barrier semaphores. Data moves between devices by JAX's collectives and lax.ppermute only.
A program may use at most 64 MiB of HBM per device.

v0:
```python
import jax
import jax.numpy as jnp
from jax import lax
from jax.sharding import PartitionSpec as P

epsilon = 1e-05
masked_score = -1e30
pair_block = 2048


def normalize(values):
    centred = values - jnp.mean(values, axis=-1, keepdims=True)
    scale = lax.rsqrt(jnp.mean(centred * centred, axis=-1, keepdims=True) + epsilon)
    return (centred * scale, scale)


def normalize_back(grad_normed, normed, scale):
    inner = grad_normed - jnp.mean(grad_normed, axis=-1, keepdims=True)
    inner = inner - normed * jnp.mean(grad_normed * normed, axis=-1, keepdims=True)
    return inner * scale


def contract_first(left, right):
    return lax.dot_general(
        left, right, (((0,), (0,)), ((), ())), preferred_element_type=jnp.float32
    )


def contract_last(left, right):
    return lax.dot_general(
        left, right, (((1,), (1,)), ((), ())), preferred_element_type=jnp.float32
    )


def bucket_flat(spatial_g, buckets):
    slots = spatial_g.shape[0]
    rows = lax.broadcasted_iota(jnp.int32, (slots, slots), 0)
    columns = lax.broadcasted_iota(jnp.int32, (slots, slots), 1)
    chosen = jnp.where((rows == 0) | (columns == 0), buckets - 1, spatial_g)
    return chosen.reshape(1, slots * slots)


def bucket_onehot(flat_ids, count, buckets):
    kinds = lax.broadcasted_iota(jnp.int32, (buckets, count), 0)
    return (flat_ids == kinds).astype(jnp.bfloat16)


def edge_counts(path_flat, start, width, edges):
    labels = lax.dynamic_slice_in_dim(path_flat, start, width, 1)
    kinds = lax.broadcasted_iota(jnp.int32, (edges, width), 0)
    total = jnp.zeros((edges, width), jnp.bfloat16)
    for hop in range(labels.shape[0]):
        total = total + (labels[hop][None, :] == kinds).astype(jnp.bfloat16)
    return total


def pair_bias(spatial_g, path_g, spatial_tab, edge_tab, start, count):
    slots = spatial_g.shape[0]
    pairs = slots * slots
    flat_ids = bucket_flat(spatial_g, spatial_tab.shape[0])
    bias = contract_first(spatial_tab, bucket_onehot(flat_ids, count, spatial_tab.shape[0]))
    path_flat = path_g.reshape(path_g.shape[0], pairs)
    width = min(count, pair_block)

    def block_terms(offset):
        return contract_first(
            edge_tab, edge_counts(path_flat, start + offset, width, edge_tab.shape[0])
        )

    terms = lax.map(block_terms, jnp.arange(count // width, dtype=jnp.int32) * width)
    terms = jnp.transpose(terms, (1, 0, 2)).reshape(bias.shape)
    return bias + terms / path_g.shape[0]


def graph_scores(query, keys, bias, count):
    slots, heads, depth = query.shape
    scores = jnp.einsum(
        "qhd,khd->hqk", query, keys, preferred_element_type=jnp.float32
    ) * depth ** (-0.5)
    scores = scores + bias.reshape(heads, slots, slots)
    places = lax.broadcasted_iota(jnp.int32, (1, 1, slots), 2)
    return jnp.where(places <= count, scores, masked_score)


def attend_graph(query, keys, values, bias, count):
    scores = graph_scores(query, keys, bias, count)
    top = jnp.max(scores, axis=-1, keepdims=True)
    weights = jnp.exp(scores - top)
    total = jnp.sum(weights, axis=-1, keepdims=True)
    probs = (weights / total).astype(jnp.bfloat16)
    attended = jnp.einsum("hqk,khd->qhd", probs, values, preferred_element_type=jnp.float32)
    return (attended.astype(jnp.bfloat16), top + jnp.log(total))


def attend_graph_back(query, keys, values, bias, count, log_total, grad_attended):
    depth = query.shape[-1]
    scores = graph_scores(query, keys, bias, count)
    probs = jnp.exp(scores - log_total)
    grad_probs = jnp.einsum(
        "qhd,khd->hqk", grad_attended, values, preferred_element_type=jnp.float32
    )
    grad_values = jnp.einsum(
        "hqk,qhd->khd",
        probs.astype(jnp.bfloat16),
        grad_attended,
        preferred_element_type=jnp.float32,
    )
    grad_scores = probs * (grad_probs - jnp.sum(probs * grad_probs, axis=-1, keepdims=True))
    grad_scores = grad_scores.astype(jnp.bfloat16)
    grad_query = jnp.einsum(
        "hqk,khd->qhd", grad_scores, keys, preferred_element_type=jnp.float32
    ) * depth ** (-0.5)
    grad_keys = jnp.einsum(
        "hqk,qhd->khd", grad_scores, query, preferred_element_type=jnp.float32
    ) * depth ** (-0.5)
    return (
        grad_query.astype(jnp.bfloat16),
        grad_keys.astype(jnp.bfloat16),
        grad_values.astype(jnp.bfloat16),
        grad_scores,
    )


def table_grads(spatial_g, path_g, piece, start, spatial_grad, edge_grad):
    count = piece.shape[1]
    pairs = spatial_g.shape[0] * spatial_g.shape[1]
    flat_ids = bucket_flat(spatial_g, spatial_grad.shape[0])
    spatial_grad = spatial_grad + contract_last(
        bucket_onehot(flat_ids, count, spatial_grad.shape[0]), piece
    )
    path_flat = path_g.reshape(path_g.shape[0], pairs)
    width = min(count, pair_block)

    def add_block(index, total):
        offset = index * width
        counts = edge_counts(path_flat, start + offset, width, edge_grad.shape[0])
        block = lax.dynamic_slice_in_dim(piece, offset, width, 1)
        return total + contract_last(counts, block)

    edge_grad = lax.fori_loop(0, count // width, add_block, edge_grad)
    return (spatial_grad, edge_grad)


def local(
    layer_in,
    node_counts,
    spatial_ids,
    path_ids,
    ln1_gain,
    ln1_bias,
    w_q,
    w_k,
    w_v,
    q_bias,
    v_bias,
    spatial_table,
    edge_table,
    w_o,
    o_bias,
    ln2_gain,
    ln2_bias,
    w_in,
    in_bias,
    w_out,
    out_bias,
    cotangent,
):
    graphs, slots = (spatial_ids.shape[0], spatial_ids.shape[1])
    pairs = slots * slots
    all_heads = spatial_table.shape[1]
    heads = all_heads // lax.axis_size("mp")
    head_width = w_q.shape[1]
    ff_width = w_in.shape[1]
    depth = head_width // heads
    split_shape = (graphs, slots, heads, depth)
    row_count = graphs * slots
    head_start = lax.axis_index("mp") * heads
    gathered = (
        lax.all_gather(w_q, "dp", axis=0, tiled=True),
        lax.all_gather(w_k, "dp", axis=0, tiled=True),
        lax.all_gather(w_v, "dp", axis=0, tiled=True),
        lax.all_gather(w_o, "dp", axis=0, tiled=True),
        lax.all_gather(w_in, "dp", axis=0, tiled=True),
        lax.all_gather(w_out, "dp", axis=0, tiled=True),
        lax.all_gather(edge_table, "dp", axis=0, tiled=True),
    )
    full_q, full_k, full_v, full_o, full_in, full_out, full_edge = gathered
    first_normed, first_scale = normalize(layer_in)
    h1 = lax.all_gather(
        (first_normed * ln1_gain + ln1_bias).astype(jnp.bfloat16), "mp", axis=0, tiled=True
    )
    query = (jnp.dot(h1, full_q, preferred_element_type=jnp.float32) + q_bias).astype(jnp.bfloat16)
    keys = jnp.dot(h1, full_k, preferred_element_type=jnp.float32).astype(jnp.bfloat16)
    values = (jnp.dot(h1, full_v, preferred_element_type=jnp.float32) + v_bias).astype(jnp.bfloat16)
    query_split = query.reshape(split_shape)
    keys_split = keys.reshape(split_shape)
    values_split = values.reshape(split_shape)
    local_spatial = lax.dynamic_slice_in_dim(spatial_table, head_start, heads, 1)
    local_edge = lax.dynamic_slice_in_dim(full_edge, head_start, heads, 1)

    def head_bias(item):
        return pair_bias(item[0], item[1], local_spatial, local_edge, 0, pairs)

    biases = lax.map(head_bias, (spatial_ids, path_ids))

    def forward_graph(item):
        query_g, keys_g, values_g, bias, count = item
        return attend_graph(query_g, keys_g, values_g, bias, count)

    attended, log_total = lax.map(
        forward_graph, (query_split, keys_split, values_split, biases, node_counts)
    )
    attended = attended.reshape(row_count, head_width)
    branch = lax.psum_scatter(
        contract_last(attended, full_o), "mp", scatter_dimension=0, tiled=True
    )
    mid = layer_in + branch + o_bias
    second_normed, second_scale = normalize(mid)
    h2 = lax.all_gather(
        (second_normed * ln2_gain + ln2_bias).astype(jnp.bfloat16), "mp", axis=0, tiled=True
    )
    pre = jnp.dot(h2, full_in, preferred_element_type=jnp.float32) + in_bias
    hidden = jax.nn.gelu(pre, approximate=False).astype(jnp.bfloat16)
    feed = lax.psum_scatter(
        contract_last(hidden, full_out).astype(jnp.bfloat16), "mp", scatter_dimension=0, tiled=True
    ).astype(jnp.float32)
    layer_out = mid + feed + out_bias
    grad_ffn = lax.all_gather(cotangent.astype(jnp.bfloat16), "mp", axis=0, tiled=True)
    grad_w_out = contract_first(grad_ffn, hidden)
    grad_hidden = jnp.dot(grad_ffn, full_out, preferred_element_type=jnp.float32)
    unused, gelu_back = jax.vjp(lambda inner: jax.nn.gelu(inner, approximate=False), pre)
    grad_pre = gelu_back(grad_hidden)[0].astype(jnp.bfloat16)
    grad_w_in = contract_first(h2, grad_pre)
    grad_h2 = lax.psum_scatter(
        contract_last(grad_pre, full_in), "mp", scatter_dimension=0, tiled=True
    )
    grad_mid = cotangent + normalize_back(grad_h2 * ln2_gain, second_normed, second_scale)
    grad_branch = lax.all_gather(grad_mid.astype(jnp.bfloat16), "mp", axis=0, tiled=True)
    grad_w_o = contract_first(grad_branch, attended)
    grad_attended = jnp.dot(grad_branch, full_o, preferred_element_type=jnp.float32).astype(
        jnp.bfloat16
    )

    def backward_graph(item):
        query_g, keys_g, values_g, bias, count, log_g, grad_g = item
        return attend_graph_back(query_g, keys_g, values_g, bias, count, log_g, grad_g)

    grad_query, grad_keys, grad_values, grad_scores = lax.map(
        backward_graph,
        (
            query_split,
            keys_split,
            values_split,
            biases,
            node_counts,
            log_total,
            grad_attended.reshape(split_shape),
        ),
    )
    score_rows = grad_scores.reshape(graphs, heads, pairs)

    def table_step(carry, item):
        spatial_g, path_g, piece = item
        return (table_grads(spatial_g, path_g, piece, table_start, carry[0], carry[1]), 0)

    table_start = 0
    start_grads = (
        jnp.zeros((spatial_table.shape[0], heads), jnp.float32),
        jnp.zeros((full_edge.shape[0], heads), jnp.float32),
    )
    table_sums, unused_steps = lax.scan(
        table_step, start_grads, (spatial_ids, path_ids, score_rows)
    )
    spatial_full = lax.dynamic_update_slice_in_dim(
        jnp.zeros((spatial_table.shape[0], all_heads), jnp.float32), table_sums[0], head_start, 1
    )
    grad_edge = table_sums[1]
    grad_edge = grad_edge / path_ids.shape[1]
    grad_query = grad_query.reshape(row_count, head_width)
    grad_keys = grad_keys.reshape(row_count, head_width)
    grad_values = grad_values.reshape(row_count, head_width)
    grad_w_q = contract_first(h1, grad_query)
    grad_w_k = contract_first(h1, grad_keys)
    grad_w_v = contract_first(h1, grad_values)
    input_terms = contract_last(grad_query, full_q) + contract_last(grad_keys, full_k)
    input_terms = input_terms + contract_last(grad_values, full_v)
    grad_h1 = lax.psum_scatter(input_terms, "mp", scatter_dimension=0, tiled=True)
    grad_layer_in = grad_mid + normalize_back(grad_h1 * ln1_gain, first_normed, first_scale)
    summed = (
        lax.psum_scatter(grad_w_q, "dp", scatter_dimension=0, tiled=True),
        lax.psum_scatter(grad_w_k, "dp", scatter_dimension=0, tiled=True),
        lax.psum_scatter(grad_w_v, "dp", scatter_dimension=0, tiled=True),
        lax.psum_scatter(grad_w_o, "dp", scatter_dimension=0, tiled=True),
        lax.psum_scatter(grad_w_in, "dp", scatter_dimension=0, tiled=True),
        lax.psum_scatter(grad_w_out, "dp", scatter_dimension=0, tiled=True),
        lax.psum_scatter(grad_edge, "dp", scatter_dimension=0, tiled=True),
    )
    model_width = layer_in.shape[1]
    feature_start = lax.axis_index("mp") * head_width
    hidden_start = lax.axis_index("mp") * ff_width
    query_full = lax.dynamic_update_slice_in_dim(
        jnp.zeros((model_width,), jnp.float32),
        jnp.sum(grad_query.astype(jnp.float32), axis=0),
        feature_start,
        0,
    )
    value_full = lax.dynamic_update_slice_in_dim(
        jnp.zeros((model_width,), jnp.float32),
        jnp.sum(grad_values.astype(jnp.float32), axis=0),
        feature_start,
        0,
    )
    hidden_full = lax.dynamic_update_slice_in_dim(
        jnp.zeros((ff_width * lax.axis_size("mp"),), jnp.float32),
        jnp.sum(grad_pre.astype(jnp.float32), axis=0),
        hidden_start,
        0,
    )
    norm_totals = lax.psum(
        (
            jnp.sum(grad_h1 * first_normed, axis=0),
            jnp.sum(grad_h1, axis=0),
            jnp.sum(grad_h2 * second_normed, axis=0),
            jnp.sum(grad_h2, axis=0),
            jnp.sum(grad_mid, axis=0),
            jnp.sum(cotangent, axis=0),
            query_full,
            value_full,
            hidden_full,
            spatial_full,
        ),
        ("dp", "mp"),
    )
    grad_q_bias = lax.dynamic_slice_in_dim(norm_totals[6], feature_start, head_width, 0)
    grad_v_bias = lax.dynamic_slice_in_dim(norm_totals[7], feature_start, head_width, 0)
    grad_in_bias = lax.dynamic_slice_in_dim(norm_totals[8], hidden_start, ff_width, 0)
    grad_spatial = lax.dynamic_slice_in_dim(norm_totals[9], head_start, heads, 1)
    return (
        layer_out,
        grad_layer_in,
        norm_totals[0],
        norm_totals[1],
        summed[0],
        summed[1],
        summed[2],
        grad_q_bias,
        grad_v_bias,
        grad_spatial,
        summed[6],
        summed[3],
        norm_totals[4],
        norm_totals[2],
        norm_totals[3],
        summed[4],
        grad_in_bias,
        summed[5],
        norm_totals[5],
    )


def solution(mesh):
    return jax.shard_map(
        local,
        mesh=mesh,
        in_specs=(
            P(("dp", "mp"), None),
            P("dp"),
            P("dp", None, None),
            P("dp", None, None, None),
            P(),
            P(),
            P("dp", "mp"),
            P("dp", "mp"),
            P("dp", "mp"),
            P("mp"),
            P("mp"),
            P(),
            P("dp", None),
            P("dp", "mp"),
            P(),
            P(),
            P(),
            P("dp", "mp"),
            P("mp"),
            P("dp", "mp"),
            P(),
            P(("dp", "mp"), None),
        ),
        out_specs=(
            P(("dp", "mp"), None),
            P(("dp", "mp"), None),
            P(),
            P(),
            P("dp", "mp"),
            P("dp", "mp"),
            P("dp", "mp"),
            P("mp"),
            P("mp"),
            P(None, "mp"),
            P("dp", "mp"),
            P("dp", "mp"),
            P(),
            P(),
            P(),
            P("dp", "mp"),
            P("mp"),
            P("dp", "mp"),
            P(),
        ),
        check_vma=False,
    )
```

profile of v0, /device:TPU:0, one launch (start us, length us, event | category | flops | bytes accessed | tf_op | source)
XLA Modules:
  0.0 1440.9 jit_solution(12586913065994715846)
XLA Ops:
  7.3 32.5 %all-gather = bf16[8,192,32]{1,2,0:T(8,128)(2,1)S(1)} all-gather(bf16[1,192,32]{1,2,0:T(8,128)(2,1)} %bitcast.346), channel_id=1, replica_groups=mesh['dp'=8,'mp'=4] {'dp'}, dimensions={0}, use_global_device_ids=true | all-gather | bytes 110592 | tf_op jit(solution)/shard_map/all_gather | solution.py:185
  40.2 307.6 %while.76 = (s32[]{:T(128)}, f32[4,8,16384]{2,1,0:T(8,128)}, s32[4,128,128]{2,1,0:T(8,128)}, bf16[22,8]{0,1:T(8,128)(2,1)S(1)}, s32[4,5,128,128]{3,2,1,0:T(8,128...) while((s32[]{:T(128)}, f32[4,8,16384]{2,1,0:T(8,128)}, ...), condition=%wide.region_5.6_spmd, body=%wide.region_2.5_spmd.sunk | while | flops 119668880 | bytes 3820008 | solution.py:204
  41.5 73.4 %while.81 = (s32[]{:T(128)}, f32[8,8,2048]{2,1,0:T(8,128)S(1)}, s32[8]{0:T(128)S(1)}, s32[5,16384]{1,0:T(8,128)S(1)}, bf16[1536,8]{0,1:T(8,128)(2,1)S(1)}, /*ind...) while((s32[]{:T(128)}, f32[8,8,2048]{2,1,0:T(8,128)S(1)}, s32[8]{0:T(128)S(1)}, ...), condition=%wide.region_4.4_spmd, body=%wide.region_3.3_spmd.sunk | while | flops 113246216 | bytes 213227 | solution.py:70
  118.4 73.4 %while.81 = (s32[]{:T(128)}, f32[8,8,2048]{2,1,0:T(8,128)S(1)}, s32[8]{0:T(128)S(1)}, s32[5,16384]{1,0:T(8,128)S(1)}, bf16[1536,8]{0,1:T(8,128)(2,1)S(1)}, /*ind...) while((s32[]{:T(128)}, f32[8,8,2048]{2,1,0:T(8,128)S(1)}, s32[8]{0:T(128)S(1)}, ...), condition=%wide.region_4.4_spmd, body=%wide.region_3.3_spmd.sunk | while | flops 113246216 | bytes 213227 | solution.py:70
  195.3 73.4 %while.81 = (s32[]{:T(128)}, f32[8,8,2048]{2,1,0:T(8,128)S(1)}, s32[8]{0:T(128)S(1)}, s32[5,16384]{1,0:T(8,128)S(1)}, bf16[1536,8]{0,1:T(8,128)(2,1)S(1)}, /*ind...) while((s32[]{:T(128)}, f32[8,8,2048]{2,1,0:T(8,128)S(1)}, s32[8]{0:T(128)S(1)}, ...), condition=%wide.region_4.4_spmd, body=%wide.region_3.3_spmd.sunk | while | flops 113246216 | bytes 213227 | solution.py:70
  272.2 73.4 %while.81 = (s32[]{:T(128)}, f32[8,8,2048]{2,1,0:T(8,128)S(1)}, s32[8]{0:T(128)S(1)}, s32[5,16384]{1,0:T(8,128)S(1)}, bf16[1536,8]{0,1:T(8,128)(2,1)S(1)}, /*ind...) while((s32[]{:T(128)}, f32[8,8,2048]{2,1,0:T(8,128)S(1)}, s32[8]{0:T(128)S(1)}, ...), condition=%wide.region_4.4_spmd, body=%wide.region_3.3_spmd.sunk | while | flops 113246216 | bytes 213227 | solution.py:70
  348.7 8.7 all_gather.33
  357.4 31.2 %all_gather.34 = bf16[768,192]{1,0:T(8,128)(2,1)S(1)} all-gather(bf16[96,192]{1,0:T(8,128)(2,1)S(1)} %copy-done.34), channel_id=1, replica_groups=mesh['dp'=8,'mp'=4] {'dp'}, dimensions={0}, use_global_device_ids=true | all-gather | bytes 331776 | tf_op jit(solution)/shard_map/all_gather | solution.py:181
  389.9 31.0 %all_gather.35 = bf16[768,192]{1,0:T(8,128)(2,1)S(1)} all-gather(bf16[96,192]{1,0:T(8,128)(2,1)S(1)} %copy-done.35), channel_id=1, replica_groups=mesh['dp'=8,'mp'=4] {'dp'}, dimensions={0}, use_global_device_ids=true | all-gather | bytes 331776 | tf_op jit(solution)/shard_map/all_gather | solution.py:179
  421.4 31.1 %all_gather.36 = bf16[768,192]{1,0:T(8,128)(2,1)S(1)} all-gather(bf16[96,192]{1,0:T(8,128)(2,1)S(1)} %copy-done.36), channel_id=1, replica_groups=mesh['dp'=8,'mp'=4] {'dp'}, dimensions={0}, use_global_device_ids=true | all-gather | bytes 331776 | tf_op jit(solution)/shard_map/all_gather | solution.py:180
  453.1 15.5 %while.77 = (s32[]{:T(128)}, bf16[4,128,8,24]{1,3,2,0:T(8,128)(2,1)S(1)}, f32[4,8,128,1]{2,1,3,0:T(8,128)}, bf16[4,128,8,24]{1,3,2,0:T(8,128)(2,1)S(1)}, s32[4]{...) while((s32[]{:T(128)}, ...), condition=%wide.region_9.10_spmd, body=%wide.region_6.9_spmd.sunk | while | flops 13786242 | bytes 5475569 | solution.py:210
  468.8 31.5 %all_gather.38 = bf16[768,192]{1,0:T(8,128)(2,1)S(1)} all-gather(bf16[96,192]{1,0:T(8,128)(2,1)S(1)} %copy-done.37), channel_id=1, replica_groups=mesh['dp'=8,'mp'=4] {'dp'}, dimensions={0}, use_global_device_ids=true | all-gather | bytes 331776 | tf_op jit(solution)/shard_map/all_gather | solution.py:182
  502.0 31.3 %all_gather.40 = bf16[768,192]{1,0:T(8,128)(2,1)S(1)} all-gather(bf16[96,192]{1,0:T(8,128)(2,1)S(1)} %copy-done.38), channel_id=1, replica_groups=mesh['dp'=8,'mp'=4] {'dp'}, dimensions={0}, use_global_device_ids=true | all-gather | bytes 331776 | tf_op jit(solution)/shard_map/all_gather | solution.py:183
  533.2 31.2 %all_gather.41 = bf16[768,192]{1,0:T(8,128)(2,1)S(1)} all-gather(bf16[96,192]{1,0:T(8,128)(2,1)} %param.53), channel_id=1, replica_groups=mesh['dp'=8,'mp'=4] {'dp'}, dimensions={0}, use_global_device_ids=true | all-gather | bytes 331776 | tf_op jit(solution)/shard_map/all_gather | solution.py:184
  565.0 7.8 all_gather.42
  575.1 8.9 all_gather.39
  592.7 26.6 %reduce-scatter.20.cloned.1.call-done = f32[128,768]{1,0:T(8,128)} async-done(((f32[512,768]{1,0:T(8,128)}), f32[128,768]{1,0:T(8,128)}) %reduce-scatter.20.cloned.1.call-update) | async-done | bytes 393232 | tf_op jit(solution)/shard_map/reduce_scatter | solution.py:234
  621.1 24.0 %reduce-scatter.18.cloned.1.call-done = bf16[128,768]{1,0:T(8,128)(2,1)} async-done(((bf16[512,768]{1,0:T(8,128)(2,1)}), bf16[128,768]{1,0:T(8,128)(2,1)}) %reduce-scatter.18.cloned.1.call-update) | async-done | bytes 196624 | tf_op jit(solution)/shard_map/reduce_scatter | solution.py:224
  647.7 8.4 all_gather.43
  657.7 26.1 %while.78 = (s32[]{:T(128)}, bf16[4,128,8,24]{1,3,2,0:T(8,128)(2,1)S(1)}, bf16[4,128,8,24]{1,3,2,0:T(8,128)(2,1)S(1)}, bf16[4,128,8,24]{1,3,2,0:T(8,128)(2,1)S(1...) while((s32[]{:T(128)}, ...), condition=%wide.region_19.20_spmd, body=%wide.region_17.19_spmd.sunk | while | flops 32889984 | bytes 9169173 | solution.py:248
  688.2 258.5 %while.80 = (s32[]{:T(128)}, f32[22,8]{0,1:T(8,128)S(1)}, f32[1536,8]{0,1:T(8,128)S(1)}, s32[4,128,128]{2,1,0:T(8,128)}, bf16[4,8,16384]{2,1,0:T(8,128)(2,1)}, /...) while((s32[]{:T(128)}, f32[22,8]{0,1:T(8,128)S(1)}, ...), condition=%wide.region_37.38_spmd.clone, body=%wide.region_34.37_spmd.clone.sunk | while | flops 119419368 | bytes 2550782 | solution.py:271
  691.8 61.1 %while.82 = (s32[]{:T(128)}, f32[1536,8]{0,1:T(8,128)S(1)}, s32[5,16384]{1,0:T(8,128)S(1)}, bf16[8,16384]{1,0:T(8,128)(2,1)S(1)}, s32[]{:T(128)}, /*index=5*/s32...) while((s32[]{:T(128)}, f32[1536,8]{0,1:T(8,128)S(1)}, s32[5,16384]{1,0:T(8,128)S(1)}, ...), condition=%wide.region_36.36_spmd, body=%wide.region_35.35_spmd.sunk | while | flops 113258504 | bytes 254187 | solution.py:140
  692.0 7.5 fusion.223
  699.6 7.5 fusion.223
  707.2 7.5 fusion.223
  714.9 7.5 fusion.223
  722.5 7.5 fusion.223
  730.2 7.5 fusion.223
  737.8 7.5 fusion.223
  745.4 7.5 fusion.223
  756.4 61.1 %while.82 = (s32[]{:T(128)}, f32[1536,8]{0,1:T(8,128)S(1)}, s32[5,16384]{1,0:T(8,128)S(1)}, bf16[8,16384]{1,0:T(8,128)(2,1)S(1)}, s32[]{:T(128)}, /*index=5*/s32...) while((s32[]{:T(128)}, f32[1536,8]{0,1:T(8,128)S(1)}, s32[5,16384]{1,0:T(8,128)S(1)}, ...), condition=%wide.region_36.36_spmd, body=%wide.region_35.35_spmd.sunk | while | flops 113258504 | bytes 254187 | solution.py:140
  756.6 7.5 fusion.223
  764.2 7.5 fusion.223
  771.8 7.5 fusion.223
  779.5 7.5 fusion.223
  787.1 7.5 fusion.223
  794.8 7.5 fusion.223
  802.4 7.5 fusion.223
  810.0 7.5 fusion.223
  821.0 61.1 %while.82 = (s32[]{:T(128)}, f32[1536,8]{0,1:T(8,128)S(1)}, s32[5,16384]{1,0:T(8,128)S(1)}, bf16[8,16384]{1,0:T(8,128)(2,1)S(1)}, s32[]{:T(128)}, /*index=5*/s32...) while((s32[]{:T(128)}, f32[1536,8]{0,1:T(8,128)S(1)}, s32[5,16384]{1,0:T(8,128)S(1)}, ...), condition=%wide.region_36.36_spmd, body=%wide.region_35.35_spmd.sunk | while | flops 113258504 | bytes 254187 | solution.py:140
  821.2 7.5 fusion.223
  828.8 7.5 fusion.223
  836.5 7.5 fusion.223
  844.1 7.5 fusion.223
  851.7 7.5 fusion.223
  859.4 7.5 fusion.223
  867.0 7.5 fusion.223
  874.6 7.5 fusion.223
  885.6 61.1 %while.82 = (s32[]{:T(128)}, f32[1536,8]{0,1:T(8,128)S(1)}, s32[5,16384]{1,0:T(8,128)S(1)}, bf16[8,16384]{1,0:T(8,128)(2,1)S(1)}, s32[]{:T(128)}, /*index=5*/s32...) while((s32[]{:T(128)}, f32[1536,8]{0,1:T(8,128)S(1)}, s32[5,16384]{1,0:T(8,128)S(1)}, ...), condition=%wide.region_36.36_spmd, body=%wide.region_35.35_spmd.sunk | while | flops 113258504 | bytes 254187 | solution.py:140
  885.8 7.5 fusion.223
  893.4 7.5 fusion.223
  901.1 7.5 fusion.223
  908.7 7.5 fusion.223
  916.3 7.5 fusion.223
  924.0 7.5 fusion.223
  962.5 48.5 %reduce-scatter.34.cloned.1.call-done = f32[192,8]{1,0:T(8,128)} async-done(((f32[1536,8]{1,0:T(8,128)}), f32[192,8]{1,0:T(8,128)}) %reduce-scatter.34.cloned.1.call-update) | async-done | bytes 6160
  1012.5 28.0 %reduce-scatter.22.cloned.1.call-done = f32[128,768]{1,0:T(8,128)} async-done(((f32[512,768]{1,0:T(8,128)}), f32[128,768]{1,0:T(8,128)}) %reduce-scatter.22.cloned.1.call-update) | async-done | bytes 393232 | tf_op jit(solution)/shard_map/reduce_scatter | solution.py:287
  1041.8 40.8 %all-reduce = (f32[768]{0:T(1024)}, f32[768]{0:T(1024)}, f32[768]{0:T(1024)S(1)}, f32[768]{0:T(1024)S(1)}, f32[22,32]{0,1:T(8,128)S(1)}, /*index=5*/f32[768]{0:T...) all-reduce(f32[768]{0:T(1024)S(1)} %get-tuple-element.487, ...), channel_id=1, replica_groups=mesh['dp'=8,'mp'=4] {'dp','mp'}, use_global_device_ids=true, to_apply=%region_24.25 | all-reduce | flops 7616 | bytes 60928 | tf_op jit(solution)/shard_map/psum | solution.py:319
  1087.0 20.0 %reduce-scatter.32.cloned.1.call-done = f32[96,192]{1,0:T(8,128)} async-done(((f32[768,192]{1,0:T(8,128)}), f32[96,192]{1,0:T(8,128)}) %reduce-scatter.32.cloned.1.call-update) | async-done | bytes 73744 | tf_op jit(solution)/shard_map/reduce_scatter | solution.py:294
  1107.1 65.4 %reduce-scatter.36.cloned.1.call-done = f32[96,192]{1,0:T(8,128)} async-done(((f32[768,192]{1,0:T(8,128)}), f32[96,192]{1,0:T(8,128)}) %reduce-scatter.36.cloned.1.call-update) | async-done | bytes 73744
  1172.4 65.7 %reduce-scatter.30.cloned.1.call-done = f32[96,192]{1,0:T(8,128)} async-done(((f32[768,192]{1,0:T(8,128)}), f32[96,192]{1,0:T(8,128)}) %reduce-scatter.30.cloned.1.call-update) | async-done | bytes 73744 | tf_op jit(solution)/shard_map/reduce_scatter | solution.py:293
  1238.1 65.3 %reduce-scatter.24.cloned.1.call-done = f32[96,192]{1,0:T(8,128)} async-done(((f32[768,192]{1,0:T(8,128)}), f32[96,192]{1,0:T(8,128)}) %reduce-scatter.24.cloned.1.call-update) | async-done | bytes 73744 | tf_op jit(solution)/shard_map/reduce_scatter | solution.py:290
  1303.4 65.5 %reduce-scatter.26.cloned.1.call-done = f32[96,192]{1,0:T(8,128)} async-done(((f32[768,192]{1,0:T(8,128)}), f32[96,192]{1,0:T(8,128)}) %reduce-scatter.26.cloned.1.call-update) | async-done | bytes 73744 | tf_op jit(solution)/shard_map/reduce_scatter | solution.py:291
  1368.9 65.4 %reduce-scatter.28.cloned.1.call-done = f32[96,192]{1,0:T(8,128)} async-done(((f32[768,192]{1,0:T(8,128)}), f32[96,192]{1,0:T(8,128)}) %reduce-scatter.28.cloned.1.call-update) | async-done | bytes 73744 | tf_op jit(solution)/shard_map/reduce_scatter | solution.py:292
  (507 shorter events, 369.4 us)
Async XLA Ops:
  7.2 32.9 %copy-start = (bf16[22,32]{1,0:T(8,128)(2,1)S(1)}, bf16[22,32]{1,0:T(8,128)(2,1)}, u32[]{:S(2)}) copy-start(bf16[22,32]{1,0:T(8,128)(2,1)} %param.45) | copy-start | bytes 4228
  7.2 565.6 %reduce-scatter.16.cloned.1.call-start = ((), (), s32[]{:S(2)}) async-start(), calls=%async_computation.11 | async-start | bytes 1966080 | tf_op jit(solution)/shard_map/reduce_scatter | solution.py:214
  40.2 307.6 %copy-start.3 = (f32[128,768]{1,0:T(8,128)S(1)}, f32[128,768]{1,0:T(8,128)}, u32[]{:S(2)}) copy-start(f32[128,768]{1,0:T(8,128)} %param.34) | copy-start | bytes 1179652
  40.2 307.9 %copy-start.40 = (f32[768]{0:T(1024)S(1)}, f32[768]{0:T(1024)}, u32[]{:S(2)}) copy-start(f32[768]{0:T(1024)} %param.38) | copy-start | bytes 9220
  40.2 307.9 %copy-start.52 = (f32[768]{0:T(1024)S(1)}, f32[768]{0:T(1024)}, u32[]{:S(2)}) copy-start(f32[768]{0:T(1024)} %param.39) | copy-start | bytes 9220
  347.8 9.6 copy-start.34
  347.8 41.6 %copy-start.56 = (f32[192]{0:T(256)S(1)}, f32[192]{0:T(256)}, u32[]{:S(2)}) copy-start(f32[192]{0:T(256)} %param.44) | copy-start | bytes 2308
  348.1 41.8 %copy-start.35 = (bf16[96,192]{1,0:T(8,128)(2,1)S(1)}, bf16[96,192]{1,0:T(8,128)(2,1)}, u32[]{:S(2)}) copy-start(bf16[96,192]{1,0:T(8,128)(2,1)} %param.40) | copy-start | bytes 110596
  348.7 72.2 %copy-start.57 = (f32[192]{0:T(256)S(1)}, f32[192]{0:T(256)}, u32[]{:S(2)}) copy-start(f32[192]{0:T(256)} %param.43) | copy-start | bytes 2308
  357.4 95.1 %copy-start.1 = (bf16[512,768]{1,0:T(8,128)(2,1)}, bf16[512,768]{1,0:T(8,128)(2,1)S(1)}, u32[]{:S(2)}) copy-start(bf16[512,768]{1,0:T(8,128)(2,1)S(1)} %all_gather.33) | copy-start | bytes 2359300
  389.4 32.0 %copy-start.36 = (bf16[96,192]{1,0:T(8,128)(2,1)S(1)}, bf16[96,192]{1,0:T(8,128)(2,1)}, u32[]{:S(2)}) copy-start(bf16[96,192]{1,0:T(8,128)(2,1)} %param.41) | copy-start | bytes 110596
  421.3 31.7 %copy-start.59 = (s32[4]{0:T(128)S(1)}, s32[4]{0:T(128)}, u32[]{:S(2)}) copy-start(s32[4]{0:T(128)} %param.35) | copy-start | bytes 52
  453.1 15.7 %copy-start.37 = (bf16[96,192]{1,0:T(8,128)(2,1)S(1)}, bf16[96,192]{1,0:T(8,128)(2,1)}, u32[]{:S(2)}) copy-start(bf16[96,192]{1,0:T(8,128)(2,1)} %param.47) | copy-start | bytes 110596
  468.6 33.3 %copy-start.31 = (bf16[4,128,8,24]{1,3,2,0:T(8,128)(2,1)}, bf16[4,128,8,24]{1,3,2,0:T(8,128)(2,1)S(1)}, u32[]{:S(2)}) copy-start(bf16[4,128,8,24]{1,3,2,0:T(8,128)(2,1)S(1)} %get-tuple-element.1186) | copy-start | bytes 589828
  468.8 64.4 %copy-start.16 = (bf16[4,128,8,24]{1,0,3,2:T(4,128)(2,1)}, bf16[4,128,8,24]{1,0,3,2:T(4,128)(2,1)S(1)}, u32[]{:S(2)}) copy-start(bf16[4,128,8,24]{1,0,3,2:T(4,128)(2,1)S(1)} %copy.108) | copy-start | bytes 589828
  468.8 33.1 %copy-start.38 = (bf16[96,192]{1,0:T(8,128)(2,1)S(1)}, bf16[96,192]{1,0:T(8,128)(2,1)}, u32[]{:S(2)}) copy-start(bf16[96,192]{1,0:T(8,128)(2,1)} %param.51) | copy-start | bytes 110596
  500.3 64.1 %copy-start.29 = (f32[128,768]{1,0:T(8,128)S(1)}, f32[128,768]{1,0:T(8,128)}, u32[]{:S(2)}) copy-start(f32[128,768]{1,0:T(8,128)} %param.55) | copy-start | bytes 1179652
  501.9 71.0 %copy-start.53 = (f32[768]{0:T(1024)S(1)}, f32[768]{0:T(1024)}, u32[]{:S(2)}) copy-start(f32[768]{0:T(1024)} %param.48) | copy-start | bytes 9220
  501.9 72.4 %copy-start.39 = (f32[768]{0:T(1024)S(1)}, f32[768]{0:T(1024)}, u32[]{:S(2)}) copy-start(f32[768]{0:T(1024)} %param.49) | copy-start | bytes 9220
  501.9 117.4 %reduce-scatter.20.cloned.1.call-start = ((), (), s32[]{:S(2)}) async-start(), calls=%async_computation.13 | async-start | bytes 1966080 | tf_op jit(solution)/shard_map/reduce_scatter | solution.py:234
  572.8 12.3 copy-start.14
  584.0 3.6 copy-start.5
  585.1 2.5 copy-start.30
  590.0 29.3 %copy-start.51 = (f32[128]{0:T(128)S(1)}, f32[128]{0:T(128)}, u32[]{:S(2)}) copy-start(f32[128]{0:T(128)} %copy-done.50) | copy-start | bytes 1540
  590.0 55.1 %copy-start.54 = (f32[768]{0:T(1024)S(1)}, f32[768]{0:T(1024)}, u32[]{:S(2)}) copy-start(f32[768]{0:T(1024)} %param.54) | copy-start | bytes 9220
  590.0 55.1 %reduce-scatter.18.cloned.1.call-start = ((), (), s32[]{:S(2)}) async-start(), calls=%async_computation.12 | async-start | bytes 983040 | tf_op jit(solution)/shard_map/reduce_scatter | solution.py:224
  591.3 53.8 %copy-start.26 = (bf16[512,192]{0,1:T(8,128)(2,1)}, bf16[512,192]{0,1:T(8,128)(2,1)S(1)}, u32[]{:S(2)}) copy-start(bf16[512,192]{0,1:T(8,128)(2,1)S(1)} %multiply_convert_fusion.1) | copy-start | bytes 589828
  592.6 418.3 %reduce-scatter.34.cloned.1.call-start = ((), (), s32[]{:S(2)}) async-start(), calls=%async_computation.20 | async-start | bytes 884736
  647.7 9.9 copy-start.10
  647.7 9.9 copy-start.60
  683.7 3.6 copy-start.22
  683.8 3.6 copy-start.24
  683.9 3.4 copy-start.18
  683.9 4.3 copy-start.55
  685.8 2.5 copy-start.20
  688.2 260.0 %copy-start.13 = (bf16[768,192]{1,0:T(8,128)(2,1)S(1)}, bf16[768,192]{1,0:T(8,128)(2,1)}, u32[]{:S(2)}) copy-start(bf16[768,192]{1,0:T(8,128)(2,1)} %copy-done.12) | copy-start | bytes 884740
  688.2 260.0 %copy-start.28 = (bf16[4,128,8,24]{1,0,3,2:T(4,128)(2,1)S(1)}, bf16[4,128,8,24]{1,0,3,2:T(4,128)(2,1)}, u32[]{:S(2)}) copy-start(bf16[4,128,8,24]{1,0,3,2:T(4,128)(2,1)} %copy.115) | copy-start | bytes 589828
  946.7 1.7 copy-start.9
  947.9 92.6 %reduce-scatter.22.cloned.1.call-start = ((), (), s32[]{:S(2)}) async-start(), calls=%async_computation.14 | async-start | bytes 1966080 | tf_op jit(solution)/shard_map/reduce_scatter | solution.py:287
  948.4 3.2 copy-start.33
  951.5 2.5 copy-start.15
  951.5 2.5 copy-start.27
  951.6 155.5 %reduce-scatter.32.cloned.1.call-start = ((), (), s32[]{:S(2)}) async-start(), calls=%async_computation.19 | async-start | bytes 884736 | tf_op jit(solution)/shard_map/reduce_scatter | solution.py:294
  954.0 1.7 copy-start.8
  954.0 1.7 copy-start.17
  954.0 218.4 %reduce-scatter.36.cloned.1.call-start = ((), (), s32[]{:S(2)}) async-start(), calls=%async_computation.21 | async-start | bytes 884736
  954.4 2.7 copy-start.2
  954.4 2.7 copy-start.21
  955.6 282.5 %reduce-scatter.30.cloned.1.call-start = ((), (), s32[]{:S(2)}) async-start(), calls=%async_computation.18 | async-start | bytes 884736 | tf_op jit(solution)/shard_map/reduce_scatter | solution.py:293
  957.1 346.3 %reduce-scatter.24.cloned.1.call-start = ((), (), s32[]{:S(2)}) async-start(), calls=%async_computation.15 | async-start | bytes 884736 | tf_op jit(solution)/shard_map/reduce_scatter | solution.py:290
  958.4 1.6 copy-start.58
  958.4 1.8 copy-start.23
  958.5 410.5 %reduce-scatter.26.cloned.1.call-start = ((), (), s32[]{:S(2)}) async-start(), calls=%async_computation.16 | async-start | bytes 884736 | tf_op jit(solution)/shard_map/reduce_scatter | solution.py:291
  959.8 2.0 copy-start.25
  959.8 80.7 %copy-start.4 = (f32[128,768]{1,0:T(8,128)S(1)}, f32[128,768]{1,0:T(8,128)}, u32[]{:S(2)}) copy-start(f32[128,768]{1,0:T(8,128)} %param.34) | copy-start | bytes 1179652
  959.8 80.7 %copy-start.41 = (f32[768]{0:T(1024)S(1)}, f32[768]{0:T(1024)}, u32[]{:S(2)}) copy-start(f32[768]{0:T(1024)} %param.38) | copy-start | bytes 9220
  959.8 80.7 %copy-start.47 = (f32[128]{0:T(128)S(1)}, f32[128]{0:T(128)}, u32[]{:S(2)}) copy-start(f32[128]{0:T(128)} %copy-done.46) | copy-start | bytes 1540
  959.8 80.7 %copy-start.49 = (f32[128]{0:T(128)S(1)}, f32[128]{0:T(128)}, u32[]{:S(2)}) copy-start(f32[128]{0:T(128)} %copy-done.48) | copy-start | bytes 1540
  959.9 81.9 %copy-start.42 = (f32[768]{0:T(1024)S(1)}, f32[768]{0:T(1024)}, u32[]{:S(2)}) copy-start(f32[768]{0:T(1024)} %get-tuple-element.606) | copy-start | bytes 9220
  959.9 81.9 %copy-start.43 = (f32[768]{0:T(1024)S(1)}, f32[768]{0:T(1024)}, u32[]{:S(2)}) copy-start(f32[768]{0:T(1024)} %get-tuple-element.485) | copy-start | bytes 9220
  959.9 81.9 %copy-start.44 = (f32[768]{0:T(1024)S(1)}, f32[768]{0:T(1024)}, u32[]{:S(2)}) copy-start(f32[768]{0:T(1024)} %get-tuple-element.491) | copy-start | bytes 9220
  959.9 81.9 %copy-start.45 = (f32[768]{0:T(1024)S(1)}, f32[768]{0:T(1024)}, u32[]{:S(2)}) copy-start(f32[768]{0:T(1024)} %get-tuple-element.588) | copy-start | bytes 9220
  959.9 125.2 %copy-start.11 = (f32[128,768]{1,0:T(8,128)S(1)}, f32[128,768]{1,0:T(8,128)}, u32[]{:S(2)}) copy-start(f32[128,768]{1,0:T(8,128)} %copy-done.10) | copy-start | bytes 1179652
  959.9 474.4 %reduce-scatter.28.cloned.1.call-start = ((), (), s32[]{:S(2)}) async-start(), calls=%async_computation.17 | async-start | bytes 884736 | tf_op jit(solution)/shard_map/reduce_scatter | solution.py:292
  (8 other events, 6.9 us)
Sparse Core Ops, SparseCore 0:
  502.0 27.9 reduce-scatter.15
  590.2 29.0 reduce-scatter.19
  621.8 23.2 reduce-scatter.17
  948.0 62.8 reduce-scatter.33
  1013.3 27.1 reduce-scatter.21
  1044.6 62.3 reduce-scatter.31
  1110.9 61.4 reduce-scatter.35
  1176.6 61.4 reduce-scatter.29
  1242.0 61.3 reduce-scatter.23
  1307.5 61.4 reduce-scatter.25
  1372.8 61.4 reduce-scatter.27
where the time goes:
time: 1440 us
  matrix products  487 us (34%)
  waiting for transfers between devices  475 us (33%)
  blocking collectives  294 us (20%)
  local copies, waits for them, and re-layouts  77.8 us (5%)
  loops' own time  63.7 us (4%)
  other arithmetic  28.2 us (2%)
  between operations  14.7 us (1%)
    dot_general x42, matrix products, contract_last(): lax.dot_general(left, right, (((1,), (1,)), ((), ())), preferred_element_...  252 us
    dot_general x42, matrix products, contract_first(): lax.dot_general(left, right, (((0,), (0,)), ((), ())), preferred_element_...  219 us
    unnamed x13, waiting for transfers between devices  114 us
    reduce_scatter x1, waiting for transfers between devices, local(): lax.psum_scatter(grad_w_o, 'dp', scatter_dimension=0, tiled=True)  65.7 us
    reduce_scatter x1, waiting for transfers between devices, local(): lax.psum_scatter(grad_w_k, 'dp', scatter_dimension=0, tiled=True)  65.5 us
    reduce_scatter x1, waiting for transfers between devices, local(): lax.psum_scatter(grad_w_v, 'dp', scatter_dimension=0, tiled=True)  65.4 us
    reduce_scatter x1, waiting for transfers between devices, local(): lax.psum_scatter(grad_w_q, 'dp', scatter_dimension=0, tiled=True)  65.3 us
    another operation x4, loops' own time, pair_bias(): lax.map(block_terms, jnp.arange(count // width, dtype=jnp.int32) * width)  62.5 us
  transfers between devices with their start and end apart: 11, of which 10 were waited for; matrix products, arithmetic and copies ran while one was open for 2% of the time, Pallas kernels for 0%

commit v1 on v0

--- a/solution.py
+++ b/solution.py
@@ -6,6 +6,28 @@
 epsilon = 1e-05
 masked_score = -1e30
 pair_block = 2048
+
+
+def in_order(pieces, dim):
+    pieces = jnp.moveaxis(pieces, 0, dim)
+    lengths = pieces.shape
+    return pieces.reshape(*lengths[:dim], lengths[dim] * lengths[dim + 1], *lengths[dim + 2 :])
+
+
+def collect(x, axis, dim):
+    peers = lax.axis_size(axis)
+    pairs = [(i, (i + 1) % peers) for i in range(peers)]
+    back = [(b, a) for a, b in pairs]
+    lower, upper = ([], [])
+    for step in range(peers - 1):
+        if step % 2 == 0:
+            lower.append(lax.ppermute(lower[-1] if lower else x, axis, pairs))
+        else:
+            upper.append(lax.ppermute(upper[-1] if upper else x, axis, back))
+    pieces = jnp.stack([*lower[::-1], x, *upper])
+    shift = lax.axis_index(axis) - len(lower)
+    pieces = pieces[(jnp.arange(peers) - shift) % peers]
+    return in_order(pieces, dim)
 
 
 def normalize(values):
@@ -182,7 +204,7 @@
         lax.all_gather(w_o, "dp", axis=0, tiled=True),
         lax.all_gather(w_in, "dp", axis=0, tiled=True),
         lax.all_gather(w_out, "dp", axis=0, tiled=True),
-        lax.all_gather(edge_table, "dp", axis=0, tiled=True),
+        collect(edge_table, "dp", 0),
     )
     full_q, full_k, full_v, full_o, full_in, full_out, full_edge = gathered
     first_normed, first_scale = normalize(layer_in)

time: 1440 us -> 1450 us (level)
  blocking collectives: 294 us -> 267 us
  starting transfers between devices: 0.68 us -> 16.3 us
    all_gather x1 -> x0, blocking collectives: 32.5 us -> none  [local(): lax.all_gather(edge_table, 'dp', axis=0, tiled=True)]
    ppermute x0 -> x7, starting transfers between devices: none -> 15.6 us  [the longest x3 12.6 us: collect(): upper.append(lax.ppermute(upper[-1] if upper else x, axis, back))]
  transfers between devices with their start and end apart: 11 -> 18, of which waited for: 10 -> 13; matrix products, arithmetic and copies ran while one was open for 2% -> 2% of each run, Pallas kernels for 0% -> 0%
where the time goes in v1:
time: 1450 us; the launch traced here: 1440 us
  matrix products  498 us (34%)
  waiting for transfers between devices  483 us (33%)
  blocking collectives  267 us (18%)
  local copies, waits for them, and re-layouts  72.3 us (5%)
  loops' own time  63.7 us (4%)
  other arithmetic  29.4 us (2%)
  starting transfers between devices  16.3 us (1%)
  between operations  14.8 us (1%)
    dot_general x42, matrix products, contract_last(): lax.dot_general(left, right, (((1,), (1,)), ((), ())), preferred_element_...  253 us
    dot_general x42, matrix products, contract_first(): lax.dot_general(left, right, (((0,), (0,)), ((), ())), preferred_element_...  219 us
    unnamed x13, waiting for transfers between devices  114 us
    reduce_scatter x1, waiting for transfers between devices, local(): lax.psum_scatter(grad_w_o, 'dp', scatter_dimension=0, tiled=True)  65.7 us
    reduce_scatter x1, waiting for transfers between devices, local(): lax.psum_scatter(grad_w_k, 'dp', scatter_dimension=0, tiled=True)  65.6 us
    reduce_scatter x1, waiting for transfers between devices, local(): lax.psum_scatter(grad_w_q, 'dp', scatter_dimension=0, tiled=True)  65.3 us
    reduce_scatter x1, waiting for transfers between devices, local(): lax.psum_scatter(grad_w_v, 'dp', scatter_dimension=0, tiled=True)  65.3 us
    another operation x4, loops' own time, pair_bias(): lax.map(block_terms, jnp.arange(count // width, dtype=jnp.int32) * width)  62.5 us
  transfers between devices with their start and end apart: 18, of which 13 were waited for; matrix products, arithmetic and copies ran while one was open for 2% of the time, Pallas kernels for 0%

profile of v1, /device:TPU:0, one launch (start us, length us, event | category | flops | bytes accessed | tf_op | source)
XLA Modules:
  0.0 1443.5 jit_solution(10700955633024108148)
XLA Ops:
  16.9 8.8 all_gather.30
  25.6 31.1 %all_gather.31 = bf16[768,192]{1,0:T(8,128)(2,1)S(1)} all-gather(bf16[96,192]{1,0:T(8,128)(2,1)S(1)} %copy-done.42), channel_id=1, replica_groups=mesh['dp'=8,'mp'=4] {'dp'}, dimensions={0}, use_global_device_ids=true | all-gather | bytes 331776 | tf_op jit(solution)/shard_map/all_gather | solution.py:203
  56.8 31.1 %all_gather.32 = bf16[768,192]{1,0:T(8,128)(2,1)S(1)} all-gather(bf16[96,192]{1,0:T(8,128)(2,1)S(1)} %copy-done.43), channel_id=1, replica_groups=mesh['dp'=8,'mp'=4] {'dp'}, dimensions={0}, use_global_device_ids=true | all-gather | bytes 331776 | tf_op jit(solution)/shard_map/all_gather | solution.py:201
  87.9 31.2 %all_gather.33 = bf16[768,192]{1,0:T(8,128)(2,1)S(1)} all-gather(bf16[96,192]{1,0:T(8,128)(2,1)S(1)} %copy-done.44), channel_id=1, replica_groups=mesh['dp'=8,'mp'=4] {'dp'}, dimensions={0}, use_global_device_ids=true | all-gather | bytes 331776 | tf_op jit(solution)/shard_map/all_gather | solution.py:202
  120.5 33.0 %all_gather.34 = bf16[768,192]{1,0:T(8,128)(2,1)} all-gather(bf16[96,192]{1,0:T(8,128)(2,1)S(1)} %copy-done.45), channel_id=1, replica_groups=mesh['dp'=8,'mp'=4] {'dp'}, dimensions={0}, use_global_device_ids=true | all-gather | bytes 331776 | tf_op jit(solution)/shard_map/all_gather | solution.py:204
  175.8 303.6 %while.76 = (s32[]{:T(128)}, f32[4,8,16384]{2,1,0:T(8,128)}, s32[4,128,128]{2,1,0:T(8,128)}, bf16[22,8]{0,1:T(8,128)(2,1)S(1)}, s32[4,5,128,128]{3,2,1,0:T(8,128...) while((s32[]{:T(128)}, f32[4,8,16384]{2,1,0:T(8,128)}, ...), condition=%wide.region_5.6_spmd, body=%wide.region_2.5_spmd.sunk | while | flops 119668880 | bytes 3820008 | solution.py:226
  176.1 73.4 %while.81 = (s32[]{:T(128)}, f32[8,8,2048]{2,1,0:T(8,128)S(1)}, s32[8]{0:T(128)S(1)}, s32[5,16384]{1,0:T(8,128)S(1)}, bf16[1536,8]{0,1:T(8,128)(2,1)S(1)}, /*ind...) while((s32[]{:T(128)}, f32[8,8,2048]{2,1,0:T(8,128)S(1)}, s32[8]{0:T(128)S(1)}, ...), condition=%wide.region_4.4_spmd, body=%wide.region_3.3_spmd.sunk | while | flops 113246216 | bytes 213227 | solution.py:92
  252.0 73.4 %while.81 = (s32[]{:T(128)}, f32[8,8,2048]{2,1,0:T(8,128)S(1)}, s32[8]{0:T(128)S(1)}, s32[5,16384]{1,0:T(8,128)S(1)}, bf16[1536,8]{0,1:T(8,128)(2,1)S(1)}, /*ind...) while((s32[]{:T(128)}, f32[8,8,2048]{2,1,0:T(8,128)S(1)}, s32[8]{0:T(128)S(1)}, ...), condition=%wide.region_4.4_spmd, body=%wide.region_3.3_spmd.sunk | while | flops 113246216 | bytes 213227 | solution.py:92
  327.9 73.4 %while.81 = (s32[]{:T(128)}, f32[8,8,2048]{2,1,0:T(8,128)S(1)}, s32[8]{0:T(128)S(1)}, s32[5,16384]{1,0:T(8,128)S(1)}, bf16[1536,8]{0,1:T(8,128)(2,1)S(1)}, /*ind...) while((s32[]{:T(128)}, f32[8,8,2048]{2,1,0:T(8,128)S(1)}, s32[8]{0:T(128)S(1)}, ...), condition=%wide.region_4.4_spmd, body=%wide.region_3.3_spmd.sunk | while | flops 113246216 | bytes 213227 | solution.py:92
  403.8 73.4 %while.81 = (s32[]{:T(128)}, f32[8,8,2048]{2,1,0:T(8,128)S(1)}, s32[8]{0:T(128)S(1)}, s32[5,16384]{1,0:T(8,128)S(1)}, bf16[1536,8]{0,1:T(8,128)(2,1)S(1)}, /*ind...) while((s32[]{:T(128)}, f32[8,8,2048]{2,1,0:T(8,128)S(1)}, s32[8]{0:T(128)S(1)}, ...), condition=%wide.region_4.4_spmd, body=%wide.region_3.3_spmd.sunk | while | flops 113246216 | bytes 213227 | solution.py:92
  479.5 16.4 %while.77 = (s32[]{:T(128)}, bf16[4,128,8,24]{1,3,2,0:T(8,128)(2,1)S(1)}, f32[4,8,128,1]{2,1,3,0:T(8,128)S(1)}, bf16[4,128,8,24]{1,3,2,0:T(8,128)(2,1)}, s32[4]{...) while((s32[]{:T(128)}, ...), condition=%wide.region_9.10_spmd, body=%wide.region_6.9_spmd.sunk | while | flops 13786242 | bytes 5475061 | solution.py:232
  497.8 31.5 %all_gather.36 = bf16[768,192]{1,0:T(8,128)(2,1)S(1)} all-gather(bf16[96,192]{1,0:T(8,128)(2,1)S(1)} %copy-done.46), channel_id=1, replica_groups=mesh['dp'=8,'mp'=4] {'dp'}, dimensions={0}, use_global_device_ids=true | all-gather | bytes 331776 | tf_op jit(solution)/shard_map/all_gather | solution.py:205
  529.4 33.0 %all_gather.37 = bf16[768,192]{1,0:T(8,128)(2,1)} all-gather(bf16[96,192]{1,0:T(8,128)(2,1)S(1)} %copy-done.47), channel_id=1, replica_groups=mesh['dp'=8,'mp'=4] {'dp'}, dimensions={0}, use_global_device_ids=true | all-gather | bytes 331776 | tf_op jit(solution)/shard_map/all_gather | solution.py:206
  564.1 9.0 all_gather.38
  574.7 8.7 all_gather.35
  592.0 25.6 %reduce-scatter.20.cloned.1.call-done = f32[128,768]{1,0:T(8,128)} async-done(((f32[512,768]{1,0:T(8,128)}), f32[128,768]{1,0:T(8,128)}) %reduce-scatter.20.cloned.1.call-update) | async-done | bytes 393232 | tf_op jit(solution)/shard_map/reduce_scatter | solution.py:256
  619.4 24.0 %reduce-scatter.18.cloned.1.call-done = bf16[128,768]{1,0:T(8,128)(2,1)} async-done(((bf16[512,768]{1,0:T(8,128)(2,1)}), bf16[128,768]{1,0:T(8,128)(2,1)}) %reduce-scatter.18.cloned.1.call-update) | async-done | bytes 196624 | tf_op jit(solution)/shard_map/reduce_scatter | solution.py:246
  646.8 8.4 all_gather.39
  657.8 30.7 %while.78 = (s32[]{:T(128)}, bf16[4,128,8,24]{1,3,2,0:T(8,128)(2,1)}, bf16[4,128,8,24]{1,3,2,0:T(8,128)(2,1)}, bf16[4,128,8,24]{1,3,2,0:T(8,128)(2,1)}, bf16[4,8...) while((s32[]{:T(128)}, ...), condition=%wide.region_19.20_spmd, body=%wide.region_17.19_spmd.sunk | while | flops 32889984 | bytes 9169173 | solution.py:270
  695.0 254.6 %while.80 = (s32[]{:T(128)}, f32[22,8]{0,1:T(8,128)S(1)}, f32[1536,8]{0,1:T(8,128)S(1)}, s32[4,128,128]{2,1,0:T(8,128)}, bf16[4,8,16384]{2,1,0:T(8,128)(2,1)}, /...) while((s32[]{:T(128)}, f32[22,8]{0,1:T(8,128)S(1)}, ...), condition=%wide.region_37.38_spmd.clone, body=%wide.region_34.37_spmd.clone.sunk | while | flops 119419368 | bytes 2550782 | solution.py:293
  697.6 61.1 %while.82 = (s32[]{:T(128)}, f32[1536,8]{0,1:T(8,128)S(1)}, s32[5,16384]{1,0:T(8,128)S(1)}, bf16[8,16384]{1,0:T(8,128)(2,1)S(1)}, s32[]{:T(128)}, /*index=5*/s32...) while((s32[]{:T(128)}, f32[1536,8]{0,1:T(8,128)S(1)}, s32[5,16384]{1,0:T(8,128)S(1)}, ...), condition=%wide.region_36.36_spmd, body=%wide.region_35.35_spmd.sunk | while | flops 113258504 | bytes 254187 | solution.py:162
  697.7 7.5 fusion.225
  705.4 7.5 fusion.225
  713.0 7.5 fusion.225
  720.6 7.5 fusion.225
  728.3 7.5 fusion.225
  735.9 7.5 fusion.225
  743.5 7.5 fusion.225
  751.2 7.5 fusion.225
  761.2 61.1 %while.82 = (s32[]{:T(128)}, f32[1536,8]{0,1:T(8,128)S(1)}, s32[5,16384]{1,0:T(8,128)S(1)}, bf16[8,16384]{1,0:T(8,128)(2,1)S(1)}, s32[]{:T(128)}, /*index=5*/s32...) while((s32[]{:T(128)}, f32[1536,8]{0,1:T(8,128)S(1)}, s32[5,16384]{1,0:T(8,128)S(1)}, ...), condition=%wide.region_36.36_spmd, body=%wide.region_35.35_spmd.sunk | while | flops 113258504 | bytes 254187 | solution.py:162
  761.4 7.5 fusion.225
  769.0 7.5 fusion.225
  776.6 7.5 fusion.225
  784.3 7.5 fusion.225
  791.9 7.5 fusion.225
  799.5 7.5 fusion.225
  807.2 7.5 fusion.225
  814.8 7.5 fusion.225
  824.8 61.1 %while.82 = (s32[]{:T(128)}, f32[1536,8]{0,1:T(8,128)S(1)}, s32[5,16384]{1,0:T(8,128)S(1)}, bf16[8,16384]{1,0:T(8,128)(2,1)S(1)}, s32[]{:T(128)}, /*index=5*/s32...) while((s32[]{:T(128)}, f32[1536,8]{0,1:T(8,128)S(1)}, s32[5,16384]{1,0:T(8,128)S(1)}, ...), condition=%wide.region_36.36_spmd, body=%wide.region_35.35_spmd.sunk | while | flops 113258504 | bytes 254187 | solution.py:162
  825.0 7.5 fusion.225
  832.6 7.5 fusion.225
  840.3 7.5 fusion.225
  847.9 7.5 fusion.225
  855.5 7.5 fusion.225
  863.2 7.5 fusion.225
  870.8 7.5 fusion.225
  878.4 7.5 fusion.225
  888.5 61.1 %while.82 = (s32[]{:T(128)}, f32[1536,8]{0,1:T(8,128)S(1)}, s32[5,16384]{1,0:T(8,128)S(1)}, bf16[8,16384]{1,0:T(8,128)(2,1)S(1)}, s32[]{:T(128)}, /*index=5*/s32...) while((s32[]{:T(128)}, f32[1536,8]{0,1:T(8,128)S(1)}, s32[5,16384]{1,0:T(8,128)S(1)}, ...), condition=%wide.region_36.36_spmd, body=%wide.region_35.35_spmd.sunk | while | flops 113258504 | bytes 254187 | solution.py:162
  888.6 7.5 fusion.225
  896.3 7.5 fusion.225
  903.9 7.5 fusion.225
  919.2 7.5 fusion.225
  926.8 7.5 fusion.225
  934.4 7.5 fusion.225
  942.1 7.5 fusion.225
  965.3 48.5 %reduce-scatter.34.cloned.1.call-done = f32[192,8]{1,0:T(8,128)} async-done(((f32[1536,8]{1,0:T(8,128)}), f32[192,8]{1,0:T(8,128)}) %reduce-scatter.34.cloned.1.call-update) | async-done | bytes 6160
  1015.3 27.9 %reduce-scatter.22.cloned.1.call-done = f32[128,768]{1,0:T(8,128)} async-done(((f32[512,768]{1,0:T(8,128)}), f32[128,768]{1,0:T(8,128)}) %reduce-scatter.22.cloned.1.call-update) | async-done | bytes 393232 | tf_op jit(solution)/shard_map/reduce_scatter | solution.py:309
  1044.6 40.8 %all-reduce = (f32[768]{0:T(1024)}, f32[768]{0:T(1024)}, f32[768]{0:T(1024)S(1)}, f32[768]{0:T(1024)S(1)}, f32[22,32]{0,1:T(8,128)S(1)}, /*index=5*/f32[768]{0:T...) all-reduce(f32[768]{0:T(1024)S(1)} %get-tuple-element.448, ...), channel_id=1, replica_groups=mesh['dp'=8,'mp'=4] {'dp','mp'}, use_global_device_ids=true, to_apply=%region_24.25 | all-reduce | flops 7616 | bytes 60928 | tf_op jit(solution)/shard_map/psum | solution.py:341
  1089.8 20.0 %reduce-scatter.32.cloned.1.call-done = f32[96,192]{1,0:T(8,128)} async-done(((f32[768,192]{1,0:T(8,128)}), f32[96,192]{1,0:T(8,128)}) %reduce-scatter.32.cloned.1.call-update) | async-done | bytes 73744 | tf_op jit(solution)/shard_map/reduce_scatter | solution.py:316
  1109.9 65.3 %reduce-scatter.36.cloned.1.call-done = f32[96,192]{1,0:T(8,128)} async-done(((f32[768,192]{1,0:T(8,128)}), f32[96,192]{1,0:T(8,128)}) %reduce-scatter.36.cloned.1.call-update) | async-done | bytes 73744
  1175.2 65.7 %reduce-scatter.30.cloned.1.call-done = f32[96,192]{1,0:T(8,128)} async-done(((f32[768,192]{1,0:T(8,128)}), f32[96,192]{1,0:T(8,128)}) %reduce-scatter.30.cloned.1.call-update) | async-done | bytes 73744 | tf_op jit(solution)/shard_map/reduce_scatter | solution.py:315
  1240.8 65.3 %reduce-scatter.24.cloned.1.call-done = f32[96,192]{1,0:T(8,128)} async-done(((f32[768,192]{1,0:T(8,128)}), f32[96,192]{1,0:T(8,128)}) %reduce-scatter.24.cloned.1.call-update) | async-done | bytes 73744 | tf_op jit(solution)/shard_map/reduce_scatter | solution.py:312
  1306.2 65.6 %reduce-scatter.26.cloned.1.call-done = f32[96,192]{1,0:T(8,128)} async-done(((f32[768,192]{1,0:T(8,128)}), f32[96,192]{1,0:T(8,128)}) %reduce-scatter.26.cloned.1.call-update) | async-done | bytes 73744 | tf_op jit(solution)/shard_map/reduce_scatter | solution.py:313
  1371.7 65.3 %reduce-scatter.28.cloned.1.call-done = f32[96,192]{1,0:T(8,128)} async-done(((f32[768,192]{1,0:T(8,128)}), f32[96,192]{1,0:T(8,128)}) %reduce-scatter.28.cloned.1.call-update) | async-done | bytes 73744 | tf_op jit(solution)/shard_map/reduce_scatter | solution.py:314
  (545 shorter events, 393.3 us)
Async XLA Ops:
  7.2 146.3 %copy-start = (bf16[22,32]{1,0:T(8,128)(2,1)S(1)}, bf16[22,32]{1,0:T(8,128)(2,1)}, u32[]{:S(2)}) copy-start(bf16[22,32]{1,0:T(8,128)(2,1)} %param.45) | copy-start | bytes 4228
  7.2 18.4 %copy-start.42 = (bf16[96,192]{1,0:T(8,128)(2,1)S(1)}, bf16[96,192]{1,0:T(8,128)(2,1)}, u32[]{:S(2)}) copy-start(bf16[96,192]{1,0:T(8,128)(2,1)} %param.42) | copy-start | bytes 110596
  7.2 49.6 %copy-start.43 = (bf16[96,192]{1,0:T(8,128)(2,1)S(1)}, bf16[96,192]{1,0:T(8,128)(2,1)}, u32[]{:S(2)}) copy-start(bf16[96,192]{1,0:T(8,128)(2,1)} %param.40) | copy-start | bytes 110596
  7.2 80.7 %copy-start.44 = (bf16[96,192]{1,0:T(8,128)(2,1)S(1)}, bf16[96,192]{1,0:T(8,128)(2,1)}, u32[]{:S(2)}) copy-start(bf16[96,192]{1,0:T(8,128)(2,1)} %param.41) | copy-start | bytes 110596
  7.2 565.8 %reduce-scatter.16.cloned.1.call-start = ((), (), s32[]{:S(2)}) async-start(), calls=%async_computation.11 | async-start | bytes 1966080 | tf_op jit(solution)/shard_map/reduce_scatter | solution.py:236
  7.3 146.2 %collective-permute-start = (bf16[192,32]{0,1:T(8,128)(2,1)}, bf16[192,32]{0,1:T(8,128)(2,1)S(1)}, u32[]{:S(2)}, u32[]{:S(2)}) collective-permute-start(bf16[192,32]{0,1:T(8,128)(2,1)} %param.46), channel_id=1, source_target_pairs={{0,4},{4,8},{8,12},{12,16},{16,20},{20,24},{24,28},{28,0},{1,5},{5... | collective-permute-start | bytes 36872 | tf_op jit(solution)/shard_map/ppermute | solution.py:24
  10.3 149.7 %collective-permute-start.4 = (bf16[192,32]{0,1:T(8,128)(2,1)}, bf16[192,32]{0,1:T(8,128)(2,1)S(1)}, u32[]{:S(2)}, u32[]{:S(2)}) collective-permute-start(bf16[192,32]{0,1:T(8,128)(2,1)} %param.46), channel_id=1, source_target_pairs={{4,0},{8,4},{12,8},{16,12},{20,16},{24,20},{28,24},{0,28},{5,1},{9... | collective-permute-start | bytes 36872 | tf_op jit(solution)/shard_map/ppermute | solution.py:26
  14.5 105.0 %copy-start.56 = (f32[128]{0:T(128)}, f32[128]{0:T(128)S(1)}, u32[]{:S(2)}) copy-start(f32[128]{0:T(128)S(1)} %broadcast_multiply_fusion.7) | copy-start | bytes 1540
  15.7 103.9 %copy-start.58 = (f32[128]{0:T(128)}, f32[128]{0:T(128)S(1)}, u32[]{:S(2)}) copy-start(f32[128]{0:T(128)S(1)} %add_rsqrt_fusion.1) | copy-start | bytes 1540
  15.7 103.9 %copy-start.63 = (f32[192]{0:T(256)S(1)}, f32[192]{0:T(256)}, u32[]{:S(2)}) copy-start(f32[192]{0:T(256)} %param.44) | copy-start | bytes 2308
  25.6 94.8 %copy-start.1 = (bf16[512,768]{1,0:T(8,128)(2,1)}, bf16[512,768]{1,0:T(8,128)(2,1)S(1)}, u32[]{:S(2)}) copy-start(bf16[512,768]{1,0:T(8,128)(2,1)S(1)} %all_gather.30) | copy-start | bytes 2359300
  25.6 94.4 %copy-start.64 = (f32[192]{0:T(256)S(1)}, f32[192]{0:T(256)}, u32[]{:S(2)}) copy-start(f32[192]{0:T(256)} %param.43) | copy-start | bytes 2308
  56.8 63.7 %copy-start.19 = (bf16[768,192]{1,0:T(8,128)(2,1)}, bf16[768,192]{1,0:T(8,128)(2,1)S(1)}, u32[]{:S(2)}) copy-start(bf16[768,192]{1,0:T(8,128)(2,1)S(1)} %all_gather.31) | copy-start | bytes 884740
  87.9 32.6 %copy-start.15 = (bf16[768,192]{1,0:T(8,128)(2,1)}, bf16[768,192]{1,0:T(8,128)(2,1)S(1)}, u32[]{:S(2)}) copy-start(bf16[768,192]{1,0:T(8,128)(2,1)S(1)} %all_gather.32) | copy-start | bytes 884740
  119.1 34.3 %copy-start.17 = (bf16[768,192]{1,0:T(8,128)(2,1)}, bf16[768,192]{1,0:T(8,128)(2,1)S(1)}, u32[]{:S(2)}) copy-start(bf16[768,192]{1,0:T(8,128)(2,1)S(1)} %all_gather.33) | copy-start | bytes 884740
  120.0 53.5 %copy-start.55 = (bf16[192,32]{0,1:T(8,128)(2,1)S(1)}, bf16[192,32]{0,1:T(8,128)(2,1)}, u32[]{:S(2)}) copy-start(bf16[192,32]{0,1:T(8,128)(2,1)} %param.46) | copy-start | bytes 36868
  153.4 22.3 %copy-start.5 = (s32[4,5,128,128]{3,2,1,0:T(8,128)S(1)}, s32[4,5,128,128]{3,2,1,0:T(8,128)}, u32[]{:S(2)}) copy-start(s32[4,5,128,128]{3,2,1,0:T(8,128)} %param.37) | copy-start | bytes 3932164
  153.5 6.5 collective-permute-start.1
  159.9 6.4 collective-permute-start.2
  160.0 8.8 collective-permute-start.5
  166.4 7.1 collective-permute-start.3
  168.8 6.1 collective-permute-start.6
  175.8 303.7 %copy-start.11 = (bf16[4,128,8,24]{1,3,2,0:T(8,128)(2,1)S(1)}, bf16[4,128,8,24]{1,3,2,0:T(8,128)(2,1)}, u32[]{:S(2)}) copy-start(bf16[4,128,8,24]{1,3,2,0:T(8,128)(2,1)} %copy.86) | copy-start | bytes 589828
  175.8 303.7 %copy-start.12 = (bf16[4,128,8,24]{1,3,2,0:T(8,128)(2,1)S(1)}, bf16[4,128,8,24]{1,3,2,0:T(8,128)(2,1)}, u32[]{:S(2)}) copy-start(bf16[4,128,8,24]{1,3,2,0:T(8,128)(2,1)} %copy.87) | copy-start | bytes 589828
  175.8 303.7 %copy-start.50 = (f32[4,8,128,1]{2,1,3,0:T(8,128)S(1)}, f32[4,8,128,1]{2,1,3,0:T(8,128)}, u32[]{:S(2)}) copy-start(f32[4,8,128,1]{2,1,3,0:T(8,128)} %custom-call.6) | copy-start | bytes 49156
  175.8 303.7 %copy-start.67 = (s32[4]{0:T(128)S(1)}, s32[4]{0:T(128)}, u32[]{:S(2)}) copy-start(s32[4]{0:T(128)} %param.35) | copy-start | bytes 52
  479.5 16.7 %copy-start.18 = (bf16[768,192]{1,0:T(8,128)(2,1)S(1)}, bf16[768,192]{1,0:T(8,128)(2,1)}, u32[]{:S(2)}) copy-start(bf16[768,192]{1,0:T(8,128)(2,1)} %all_gather.34) | copy-start | bytes 884740
  496.1 66.2 %copy-start.23 = (bf16[4,128,8,24]{1,0,3,2:T(4,128)(2,1)}, bf16[4,128,8,24]{1,0,3,2:T(4,128)(2,1)S(1)}, u32[]{:S(2)}) copy-start(bf16[4,128,8,24]{1,0,3,2:T(4,128)(2,1)S(1)} %copy.88) | copy-start | bytes 589828
  496.1 33.2 %copy-start.47 = (bf16[96,192]{1,0:T(8,128)(2,1)S(1)}, bf16[96,192]{1,0:T(8,128)(2,1)}, u32[]{:S(2)}) copy-start(bf16[96,192]{1,0:T(8,128)(2,1)} %param.53) | copy-start | bytes 110596
  497.7 75.3 %copy-start.3 = (f32[128,768]{1,0:T(8,128)S(1)}, f32[128,768]{1,0:T(8,128)}, u32[]{:S(2)}) copy-start(f32[128,768]{1,0:T(8,128)} %param.34) | copy-start | bytes 1179652
  497.7 75.3 %copy-start.60 = (f32[768]{0:T(1024)S(1)}, f32[768]{0:T(1024)}, u32[]{:S(2)}) copy-start(f32[768]{0:T(1024)} %param.48) | copy-start | bytes 9220
  497.7 76.8 %copy-start.48 = (f32[768]{0:T(1024)S(1)}, f32[768]{0:T(1024)}, u32[]{:S(2)}) copy-start(f32[768]{0:T(1024)} %param.49) | copy-start | bytes 9220
  497.8 76.8 %copy-start.61 = (f32[768]{0:T(1024)S(1)}, f32[768]{0:T(1024)}, u32[]{:S(2)}) copy-start(f32[768]{0:T(1024)} %param.50) | copy-start | bytes 9220
  497.8 119.8 %reduce-scatter.20.cloned.1.call-start = ((), (), s32[]{:S(2)}) async-start(), calls=%async_computation.13 | async-start | bytes 1966080 | tf_op jit(solution)/shard_map/reduce_scatter | solution.py:256
  564.1 19.3 %copy-start.66 = (f32[192]{0:T(256)S(1)}, f32[192]{0:T(256)}, u32[]{:S(2)}) copy-start(f32[192]{0:T(256)} %param.52) | copy-start | bytes 2308
  573.1 10.8 copy-start.21
  573.1 10.8 copy-start.37
  587.1 3.5 copy-start.38
  588.7 54.8 %copy-start.36 = (f32[128,768]{1,0:T(8,128)S(1)}, f32[128,768]{1,0:T(8,128)}, u32[]{:S(2)}) copy-start(f32[128,768]{1,0:T(8,128)} %param.55) | copy-start | bytes 1179652
  588.7 54.8 %copy-start.62 = (f32[768]{0:T(1024)S(1)}, f32[768]{0:T(1024)}, u32[]{:S(2)}) copy-start(f32[768]{0:T(1024)} %param.54) | copy-start | bytes 9220
  588.7 54.7 %reduce-scatter.18.cloned.1.call-start = ((), (), s32[]{:S(2)}) async-start(), calls=%async_computation.12 | async-start | bytes 983040 | tf_op jit(solution)/shard_map/reduce_scatter | solution.py:246
  592.0 421.8 %reduce-scatter.34.cloned.1.call-start = ((), (), s32[]{:S(2)}) async-start(), calls=%async_computation.20 | async-start | bytes 884736
  688.5 3.9 copy-start.29
  688.5 4.1 copy-start.16
  689.6 4.5 copy-start.25
  689.6 4.5 copy-start.31
  694.9 256.1 %copy-start.20 = (bf16[768,192]{1,0:T(8,128)(2,1)S(1)}, bf16[768,192]{1,0:T(8,128)(2,1)}, u32[]{:S(2)}) copy-start(bf16[768,192]{1,0:T(8,128)(2,1)} %copy-done.19) | copy-start | bytes 884740
  694.9 256.1 %copy-start.35 = (bf16[4,128,8,24]{1,0,3,2:T(4,128)(2,1)S(1)}, bf16[4,128,8,24]{1,0,3,2:T(4,128)(2,1)}, u32[]{:S(2)}) copy-start(bf16[4,128,8,24]{1,0,3,2:T(4,128)(2,1)} %copy.95) | copy-start | bytes 589828
  950.8 92.5 %reduce-scatter.22.cloned.1.call-start = ((), (), s32[]{:S(2)}) async-start(), calls=%async_computation.14 | async-start | bytes 1966080 | tf_op jit(solution)/shard_map/reduce_scatter | solution.py:309
  954.4 155.5 %reduce-scatter.32.cloned.1.call-start = ((), (), s32[]{:S(2)}) async-start(), calls=%async_computation.19 | async-start | bytes 884736 | tf_op jit(solution)/shard_map/reduce_scatter | solution.py:316
  956.8 218.3 %reduce-scatter.36.cloned.1.call-start = ((), (), s32[]{:S(2)}) async-start(), calls=%async_computation.21 | async-start | bytes 884736
  958.4 282.4 %reduce-scatter.30.cloned.1.call-start = ((), (), s32[]{:S(2)}) async-start(), calls=%async_computation.18 | async-start | bytes 884736 | tf_op jit(solution)/shard_map/reduce_scatter | solution.py:315
  959.9 346.3 %reduce-scatter.24.cloned.1.call-start = ((), (), s32[]{:S(2)}) async-start(), calls=%async_computation.15 | async-start | bytes 884736 | tf_op jit(solution)/shard_map/reduce_scatter | solution.py:312
  961.3 410.4 %reduce-scatter.26.cloned.1.call-start = ((), (), s32[]{:S(2)}) async-start(), calls=%async_computation.16 | async-start | bytes 884736 | tf_op jit(solution)/shard_map/reduce_scatter | solution.py:313
  962.7 80.6 %copy-start.4 = (f32[128,768]{1,0:T(8,128)S(1)}, f32[128,768]{1,0:T(8,128)}, u32[]{:S(2)}) copy-start(f32[128,768]{1,0:T(8,128)} %param.34) | copy-start | bytes 1179652
  962.7 80.6 %copy-start.49 = (f32[768]{0:T(1024)S(1)}, f32[768]{0:T(1024)}, u32[]{:S(2)}) copy-start(f32[768]{0:T(1024)} %param.38) | copy-start | bytes 9220
  962.7 80.6 %copy-start.57 = (f32[128]{0:T(128)S(1)}, f32[128]{0:T(128)}, u32[]{:S(2)}) copy-start(f32[128]{0:T(128)} %copy-done.56) | copy-start | bytes 1540
  962.7 80.6 %copy-start.59 = (f32[128]{0:T(128)S(1)}, f32[128]{0:T(128)}, u32[]{:S(2)}) copy-start(f32[128]{0:T(128)} %copy-done.58) | copy-start | bytes 1540
  962.7 81.8 %copy-start.51 = (f32[768]{0:T(1024)S(1)}, f32[768]{0:T(1024)}, u32[]{:S(2)}) copy-start(f32[768]{0:T(1024)} %get-tuple-element.567) | copy-start | bytes 9220
  962.7 81.8 %copy-start.52 = (f32[768]{0:T(1024)S(1)}, f32[768]{0:T(1024)}, u32[]{:S(2)}) copy-start(f32[768]{0:T(1024)} %get-tuple-element.446) | copy-start | bytes 9220
  962.7 81.8 %copy-start.53 = (f32[768]{0:T(1024)S(1)}, f32[768]{0:T(1024)}, u32[]{:S(2)}) copy-start(f32[768]{0:T(1024)} %get-tuple-element.452) | copy-start | bytes 9220
  962.8 81.8 %copy-start.54 = (f32[768]{0:T(1024)S(1)}, f32[768]{0:T(1024)}, u32[]{:S(2)}) copy-start(f32[768]{0:T(1024)} %get-tuple-element.549) | copy-start | bytes 9220
  962.8 125.1 %copy-start.14 = (f32[128,768]{1,0:T(8,128)S(1)}, f32[128,768]{1,0:T(8,128)}, u32[]{:S(2)}) copy-start(f32[128,768]{1,0:T(8,128)} %copy-done.13) | copy-start | bytes 1179652
  962.8 474.2 %reduce-scatter.28.cloned.1.call-start = ((), (), s32[]{:S(2)}) async-start(), calls=%async_computation.17 | async-start | bytes 884736 | tf_op jit(solution)/shard_map/reduce_scatter | solution.py:314
  (22 other events, 42.7 us)
Sparse Core Ops, SparseCore 0:
  497.9 29.4 reduce-scatter.15
  588.8 28.7 reduce-scatter.19
  620.1 23.2 reduce-scatter.17
  950.9 62.8 reduce-scatter.33
  1016.1 27.0 reduce-scatter.21
  1047.4 62.4 reduce-scatter.31
  1113.7 61.3 reduce-scatter.35
  1179.4 61.3 reduce-scatter.29
  1244.7 61.4 reduce-scatter.23
  1310.2 61.4 reduce-scatter.25
  1375.6 61.3 reduce-scatter.27
